TPU v7x, 32 devices: a whole 2x2x4 slice. The times are simulated.
32 devices in a mesh: outer: 8 (over z, y), inner: 4 (over x, core).
Axes of the slice: x: 2, y: 2, z: 4, core: 2. Of those that a mesh axis runs over, the one named last changes fastest.
Arguments:
- query_states: bfloat16 [4096, 4096], P(('outer', 'inner')), may hold values from -6 to 6
- key_states: bfloat16 [4096, 4096], P(('outer', 'inner')), may hold values from -6 to 6
- value_states: bfloat16 [4096, 4096], P(('outer', 'inner')), may hold values from -6 to 6
- doc_lengths: int32 [8], replicated, may hold values from 1 to 1024, 4096 in all
- slopes: float32 [32], replicated, may hold values from 0.00024414062 to 0.0625
Outputs:
- attended: bfloat16 [4096, 4096], P(('outer', 'inner'))
Inputs may be any that keep to these rules, and one draw needn't show every extreme that they name: `doc_lengths`: the lengths add up to 4096; the longest is exactly 1024.
All inputs are finite; a program needn't handle non-finite values.
Results may differ from a plain program's by a relative error of at most 0.0045.
Values may be sent and summed in bfloat16 or wider, within the bound.
A program may use at most 64 MiB of HBM per device.

v0:
```python
import functools
import math

import jax
import jax.numpy as jnp
from jax import lax
from jax.experimental import pallas as pl
from jax.experimental.pallas import tpu as pltpu
from jax.sharding import PartitionSpec as P

DOC_MAX = 1024
BLOCK = 256
NEG_FILL = -1e30
LOG2E = math.log2(math.e)
MESH = pl.DeviceIdType.MESH


def kernel(
    plane_groups, inner_count, planes, heads, width,
    doc_hbm, slope_hbm, q_ref, k_ref, v_ref, out_ref,
    doc_ref, slope_ref, q_buf, k_buf, v_buf, vt_buf, o_buf,
    far_out, far_in, lse_out, lse_in, near_sum, near_max, near_total, start_buf, pos_buf,
    small_sem, in_send, in_recv, z_send, z_recv, out_send, out_recv,
):
    rows = q_ref.shape[0]
    slots = plane_groups * inner_count
    outer = lax.axis_index("outer")
    inner = lax.axis_index("inner")
    plane = outer // plane_groups
    slot = (outer % plane_groups) * inner_count + inner
    has_prev = plane > 0
    has_next = plane < planes - 1
    prev_id = {"outer": outer - plane_groups, "inner": inner}
    next_id = {"outer": outer + plane_groups, "inner": inner}

    def device_of(peer):
        return {"outer": plane * plane_groups + peer // inner_count, "inner": peer % inner_count}

    def columns(owner, head):
        return pl.ds(pl.multiple_of((owner * heads + head) * width, width), width)

    own_rows = pl.ds(pl.multiple_of(slot * rows, rows), rows)

    small = [
        pltpu.make_async_copy(doc_hbm, doc_ref, small_sem.at[0]),
        pltpu.make_async_copy(slope_hbm, slope_ref, small_sem.at[1]),
    ]
    for copy in small:
        copy.start()

    barrier = pltpu.get_barrier_semaphore()
    for step in range(1, slots):
        pl.semaphore_signal(
            barrier, inc=1, device_id=device_of((slot + step) % slots), device_id_type=MESH
        )

    @pl.when(has_prev)
    def _():
        pl.semaphore_signal(barrier, inc=1, device_id=prev_id, device_id_type=MESH)

    @pl.when(has_next)
    def _():
        pl.semaphore_signal(barrier, inc=1, device_id=next_id, device_id_type=MESH)

    pl.semaphore_wait(barrier, slots - 1 + has_prev.astype(jnp.int32) + has_next.astype(jnp.int32))

    def exchange(kind, source, target, head):
        for step in range(1, slots):
            peer = (slot + step) % slots
            pltpu.make_async_remote_copy(
                src_ref=source.at[:, columns(peer, head)],
                dst_ref=target.at[head, own_rows, :],
                send_sem=in_send.at[kind],
                recv_sem=in_recv.at[kind, head],
                device_id=device_of(peer),
                device_id_type=MESH,
            ).start()
        pltpu.make_async_copy(
            source.at[:, columns(slot, head)], target.at[head, own_rows, :], in_recv.at[kind, head]
        ).start()

    for head in range(heads):
        exchange(0, q_ref, q_buf, head)
    for head in range(heads):
        exchange(1, k_ref, k_buf, head)
        exchange(2, v_ref, v_buf, head)

    for copy in small:
        copy.wait()

    position = plane * DOC_MAX + lax.broadcasted_iota(jnp.int32, (1, 2 * DOC_MAX), 1)

    def next_document(index, carry):
        end, start = carry
        end = end + doc_ref[index]
        return end, jnp.where(position >= end, end, start)

    start = lax.fori_loop(
        0, doc_ref.shape[0], next_document, (jnp.int32(0), jnp.zeros((1, 2 * DOC_MAX), jnp.int32))
    )[1]
    start_buf[...] = (start - plane * DOC_MAX).astype(jnp.float32)
    pos_buf[...] = lax.broadcasted_iota(jnp.int32, (DOC_MAX, BLOCK), 0).astype(jnp.float32)

    def whole(ref, sem):
        return pltpu.make_async_copy(ref, ref, sem)

    def z_copy(kind, head, index, source, target, device_id):
        return pltpu.make_async_remote_copy(
            src_ref=source,
            dst_ref=target,
            send_sem=z_send.at[kind, head, index],
            recv_sem=z_recv.at[kind, head, index],
            device_id=device_id,
            device_id_type=MESH,
        )

    scale = LOG2E / math.sqrt(width)
    blocks = DOC_MAX // BLOCK

    def score(head, query_first, key_first, key_count, slope, shift):
        keys = k_buf[head, pl.ds(key_first, key_count), :]
        query = q_buf[head, pl.ds(query_first, BLOCK), :]
        product = lax.dot_general(
            keys, query, (((1,), (1,)), ((), ())), preferred_element_type=jnp.float32
        )
        key_pos = pos_buf[pl.ds(key_first, key_count), :]
        allowed = key_pos >= start_buf[:, pl.ds(query_first, BLOCK)]
        return product * scale + (slope * key_pos + shift), allowed

    def weighted(key_first, key_count, weights):
        return jnp.dot(
            vt_buf[:, pl.ds(key_first, key_count)],
            weights.astype(jnp.bfloat16),
            preferred_element_type=jnp.float32,
        )

    def far(head, slope):
        for index in range(blocks):
            first, count = index * BLOCK, DOC_MAX - index * BLOCK
            scores, allowed = score(head, DOC_MAX + first, first, count, slope, -DOC_MAX * slope)
            scores = jnp.where(allowed, scores, NEG_FILL)
            row_max = jnp.max(scores, axis=0, keepdims=True)
            weights = jnp.exp2(scores - row_max)
            row_total = jnp.sum(weights, axis=0, keepdims=True)
            part = weighted(first, count, weights) / row_total
            far_out[head, index] = part.astype(far_out.dtype)
            lse_out[head, index] = row_max + jnp.log2(row_total)
            z_copy(1, head, index, far_out.at[head, index], far_in.at[head, index], next_id).start()
            z_copy(2, head, index, lse_out.at[head, index], lse_in.at[head, index], next_id).start()

    def near(head, slope):
        for index in range(blocks):
            first = index * BLOCK
            scores, allowed = score(head, first, first, BLOCK, slope, 0.0)
            causal = lax.broadcasted_iota(jnp.int32, (BLOCK, BLOCK), 0) <= (
                lax.broadcasted_iota(jnp.int32, (BLOCK, BLOCK), 1)
            )
            pieces = [(first, BLOCK, jnp.where(allowed & causal, scores, NEG_FILL))]
            if index:
                scores, allowed = score(head, first, 0, first, slope, 0.0)
                pieces.append((0, first, jnp.where(allowed, scores, NEG_FILL)))
            row_max = functools.reduce(
                jnp.maximum, [jnp.max(piece, axis=0, keepdims=True) for _, _, piece in pieces]
            )
            row_total, total = 0.0, 0.0
            for key_first, key_count, piece in pieces:
                weights = jnp.exp2(piece - row_max)
                row_total = row_total + jnp.sum(weights, axis=0, keepdims=True)
                total = total + weighted(key_first, key_count, weights)
            near_sum[:, pl.ds(first, BLOCK)] = total
            near_max[:, pl.ds(first, BLOCK)] = row_max
            near_total[:, pl.ds(first, BLOCK)] = row_total

    def send_home(head, index):
        for part in range(BLOCK // rows):
            peer = index * (BLOCK // rows) + part
            done_rows = o_buf.at[head, pl.ds(peer * rows, rows), :]

            @pl.when(peer != slot)
            def _():
                pltpu.make_async_remote_copy(
                    src_ref=done_rows,
                    dst_ref=out_ref.at[:, columns(slot, head)],
                    send_sem=out_send,
                    recv_sem=out_recv,
                    device_id=device_of(peer),
                    device_id_type=MESH,
                ).start()

            @pl.when(peer == slot)
            def _():
                pltpu.make_async_copy(
                    done_rows, out_ref.at[:, columns(slot, head)], out_recv
                ).start()

    def finish(head, send):
        for index in range(blocks):
            part = pl.ds(index * BLOCK, BLOCK)

            @pl.when(has_prev)
            def _():
                whole(far_in.at[head, index], z_recv.at[1, head, index]).wait()
                whole(lse_in.at[head, index], z_recv.at[2, head, index]).wait()
                far_lse = lse_in[head, index]
                top = jnp.maximum(near_max[:, part], far_lse)
                near_scale = jnp.exp2(near_max[:, part] - top)
                far_scale = jnp.exp2(far_lse - top)
                inverse = 1.0 / (near_total[:, part] * near_scale + far_scale)
                merged = near_sum[:, part] * (near_scale * inverse)
                merged = merged + far_in[head, index].astype(jnp.float32) * (far_scale * inverse)
                o_buf[head, part, :] = merged.T.astype(o_buf.dtype)

            @pl.when(jnp.logical_not(has_prev))
            def _():
                alone = near_sum[:, part] / near_total[:, part]
                o_buf[head, part, :] = alone.T.astype(o_buf.dtype)

            if send:
                send_home(head, index)

    def queries_back(head, unused):
        whole(q_buf.at[head, pl.ds(0, DOC_MAX), :], in_recv.at[0, head]).wait()

        @pl.when(has_prev)
        def _():
            z_copy(
                0, head, 0,
                q_buf.at[head, pl.ds(0, DOC_MAX), :],
                q_buf.at[head, pl.ds(DOC_MAX, DOC_MAX), :],
                prev_id,
            ).start()

        return unused

    lax.fori_loop(0, heads, queries_back, 0)

    def one_head(head, unused):
        slope = slope_ref[slot * heads + head] * LOG2E
        whole(k_buf.at[head], in_recv.at[1, head]).wait()
        whole(v_buf.at[head], in_recv.at[2, head]).wait()

        @pl.when(head == heads - 1)
        def _():
            def send_early(early, unused):
                for index in range(blocks):
                    send_home(early, index)
                return unused

            lax.fori_loop(0, heads - 2, send_early, 0)

        vt_buf[...] = v_buf[head].T

        @pl.when(has_next)
        def _():
            whole(q_buf.at[head, pl.ds(DOC_MAX, DOC_MAX), :], z_recv.at[0, head, 0]).wait()
            far(head, slope)

        @pl.when(head > 0)
        def _():
            finish(head - 1, False)

        @pl.when(head == heads - 1)
        def _():
            for index in range(blocks):
                send_home(heads - 2, index)

        near(head, slope)
        return unused

    lax.fori_loop(0, heads, one_head, 0)
    finish(heads - 1, True)

    sent = pl.ds(0, (slots - 1) * heads * width)
    for kind, source in enumerate((q_ref, k_ref, v_ref)):
        whole(source.at[:, sent], in_send.at[kind]).wait()
    whole(out_ref.at[:, sent], out_send).wait()
    for head in range(heads):

        @pl.when(has_prev)
        def _():
            whole(q_buf.at[head, pl.ds(0, DOC_MAX), :], z_send.at[0, head, 0]).wait()

        @pl.when(has_next)
        def _():
            for index in range(blocks):
                whole(far_out.at[head, index], z_send.at[1, head, index]).wait()
                whole(lse_out.at[head, index], z_send.at[2, head, index]).wait()

    whole(out_ref, out_recv).wait()


def per_device(query_states, key_states, value_states, doc_lengths, slopes):
    rows, all_columns = query_states.shape
    width = all_columns // slopes.shape[0]
    inner_count = lax.axis_size("inner")
    plane_groups = DOC_MAX // (rows * inner_count)
    slots = plane_groups * inner_count
    planes = lax.axis_size("outer") // plane_groups
    heads = slopes.shape[0] // slots
    blocks = DOC_MAX // BLOCK
    dtype = query_states.dtype
    return pl.pallas_call(
        functools.partial(kernel, plane_groups, inner_count, planes, heads, width),
        out_shape=jax.ShapeDtypeStruct((rows, all_columns), dtype),
        in_specs=[pl.BlockSpec(memory_space=pltpu.HBM)] * 5,
        out_specs=pl.BlockSpec(memory_space=pltpu.HBM),
        scratch_shapes=[
            pltpu.SMEM(doc_lengths.shape, doc_lengths.dtype),
            pltpu.SMEM(slopes.shape, slopes.dtype),
            pltpu.VMEM((heads, 2 * DOC_MAX, width), dtype),
            pltpu.VMEM((heads, DOC_MAX, width), dtype),
            pltpu.VMEM((heads, DOC_MAX, width), dtype),
            pltpu.VMEM((width, DOC_MAX), dtype),
            pltpu.VMEM((heads, DOC_MAX, width), dtype),
            pltpu.VMEM((heads, blocks, width, BLOCK), dtype),
            pltpu.VMEM((heads, blocks, width, BLOCK), dtype),
            pltpu.VMEM((heads, blocks, 1, BLOCK), jnp.float32),
            pltpu.VMEM((heads, blocks, 1, BLOCK), jnp.float32),
            pltpu.VMEM((width, DOC_MAX), jnp.float32),
            pltpu.VMEM((1, DOC_MAX), jnp.float32),
            pltpu.VMEM((1, DOC_MAX), jnp.float32),
            pltpu.VMEM((1, 2 * DOC_MAX), jnp.float32),
            pltpu.VMEM((DOC_MAX, BLOCK), jnp.float32),
            pltpu.SemaphoreType.DMA((2,)),
            pltpu.SemaphoreType.DMA((3,)),
            pltpu.SemaphoreType.DMA((3, heads)),
            pltpu.SemaphoreType.DMA((3, heads, blocks)),
            pltpu.SemaphoreType.DMA((3, heads, blocks)),
            pltpu.SemaphoreType.DMA,
            pltpu.SemaphoreType.DMA,
        ],
        compiler_params=pltpu.CompilerParams(
            collective_id=0, has_side_effects=True, vmem_limit_bytes=64 * 1024 * 1024
        ),
        cost_estimate=pl.CostEstimate(
            flops=4 * heads * DOC_MAX * (DOC_MAX + BLOCK) * width,
            bytes_accessed=8 * rows * all_columns,
            transcendentals=heads * DOC_MAX * (DOC_MAX + BLOCK),
        ),
    )(doc_lengths, slopes, query_states, key_states, value_states)


def solution(mesh):
    placed = P(("outer", "inner"), None)
    return jax.shard_map(
        per_device,
        mesh=mesh,
        in_specs=(placed, placed, placed, P(), P()),
        out_specs=placed,
        check_vma=False,
    )
```

profile of v0, /device:TPU:1, one launch (start us, length us, event | category | flops | bytes accessed | tf_op | source)
XLA Modules:
  0.0 55.7 jit_solution(299861582754382126)
XLA Ops:
  0.0 53.5 %shard_map.55 = bf16[128,4096]{1,0:T(8,128)(2,1)} custom-call(s32[8]{0:T(128)} %doc_hbm.1, f32[32]{0:T(128)} %slope_hbm.1, bf16[128,4096]{1,0:T(8,128)(2,1)} %q_ref.1, bf16[128,4096]{1,0:T(8,128)(2,1)} %k_ref.1, bf16[128,4096]{1,0:T(8,128)(2,1)} %v_ref.1), custom_call_target="tpu_custom_call" | custom-call | flops 2684354560 | bytes 4194304 | tf_op jit(solution)/shard_map/pallas_call | solution.py:302
  53.5 2.3 %copy.7 = bf16[128,4096]{1,0:T(8,128)(2,1)} copy(bf16[128,4096]{1,0:T(8,128)(2,1)} %shard_map.55) | data formatting | bytes 2097152
where the time goes:
time: 55.9 us; the launch traced here: 55.7 us
  Pallas kernels  53.5 us (96%)
  local copies, waits for them, and re-layouts  2.29 us (4%)
    pallas_call x1, Pallas kernels, per_device(): pl.pallas_call(functools.partial(kernel, plane_groups, inner_count, plane...  53.5 us
    unnamed x1, local copies, waits for them, and re-layouts  2.29 us

commit v1 on v0

--- a/solution.py
+++ b/solution.py
@@ -19,7 +19,7 @@
     plane_groups, inner_count, planes, heads, width,
     doc_hbm, slope_hbm, q_ref, k_ref, v_ref, out_ref,
     doc_ref, slope_ref, q_buf, k_buf, v_buf, vt_buf, o_buf,
-    far_out, far_in, lse_out, lse_in, near_sum, near_max, near_total, start_buf, pos_buf,
+    far_out, far_in, lse_out, lse_in, near_sum, near_max, near_total, far_weights, near_weights, far_inverse, start_buf, pos_buf,
     small_sem, in_send, in_recv, z_send, z_recv, out_send, out_recv,
 ):
     rows = q_ref.shape[0]
@@ -36,6 +36,16 @@
     def device_of(peer):
         return {"outer": plane * plane_groups + peer // inner_count, "inner": peer % inner_count}
 
+    def partner(step):
+        peer, unit = 0, 1
+        while unit < slots:
+            peer = peer + (slot // unit + step // unit) % 2 * unit
+            unit = 2 * unit
+        return peer
+
+    peers = [partner(step) for step in sorted(range(1, slots), key=lambda step: (step % 2, step))]
+    peers = peers[: slots // 2 - 1] + peers[slots // 2 :] + peers[slots // 2 - 1 : slots // 2]
+
     def columns(owner, head):
         return pl.ds(pl.multiple_of((owner * heads + head) * width, width), width)
 
@@ -49,10 +59,8 @@
         copy.start()
 
     barrier = pltpu.get_barrier_semaphore()
-    for step in range(1, slots):
-        pl.semaphore_signal(
-            barrier, inc=1, device_id=device_of((slot + step) % slots), device_id_type=MESH
-        )
+    for peer in peers:
+        pl.semaphore_signal(barrier, inc=1, device_id=device_of(peer), device_id_type=MESH)
 
     @pl.when(has_prev)
     def _():
@@ -65,8 +73,7 @@
     pl.semaphore_wait(barrier, slots - 1 + has_prev.astype(jnp.int32) + has_next.astype(jnp.int32))
 
     def exchange(kind, source, target, head):
-        for step in range(1, slots):
-            peer = (slot + step) % slots
+        for peer in peers:
             pltpu.make_async_remote_copy(
                 src_ref=source.at[:, columns(peer, head)],
                 dst_ref=target.at[head, own_rows, :],
@@ -129,12 +136,16 @@
 
     def weighted(key_first, key_count, weights):
         return jnp.dot(
-            vt_buf[:, pl.ds(key_first, key_count)],
-            weights.astype(jnp.bfloat16),
-            preferred_element_type=jnp.float32,
+            vt_buf[:, pl.ds(key_first, key_count)], weights, preferred_element_type=jnp.float32
         )
 
-    def far(head, slope):
+    def far_place(index):
+        return pl.ds(index * DOC_MAX - index * (index - 1) // 2 * BLOCK, DOC_MAX - index * BLOCK)
+
+    def near_place(index):
+        return index * (index + 1) // 2 * BLOCK
+
+    def far_weigh(head, slope):
         for index in range(blocks):
             first, count = index * BLOCK, DOC_MAX - index * BLOCK
             scores, allowed = score(head, DOC_MAX + first, first, count, slope, -DOC_MAX * slope)
@@ -142,34 +153,46 @@
             row_max = jnp.max(scores, axis=0, keepdims=True)
             weights = jnp.exp2(scores - row_max)
             row_total = jnp.sum(weights, axis=0, keepdims=True)
-            part = weighted(first, count, weights) / row_total
+            far_weights[far_place(index), :] = weights.astype(far_weights.dtype)
+            far_inverse[:, pl.ds(first, BLOCK)] = 1.0 / row_total
+            lse_out[head, index] = row_max + jnp.log2(row_total)
+
+    def far_send(head):
+        for index in range(blocks):
+            first, count = index * BLOCK, DOC_MAX - index * BLOCK
+            part = weighted(first, count, far_weights[far_place(index), :])
+            part = part * far_inverse[:, pl.ds(first, BLOCK)]
             far_out[head, index] = part.astype(far_out.dtype)
-            lse_out[head, index] = row_max + jnp.log2(row_total)
             z_copy(1, head, index, far_out.at[head, index], far_in.at[head, index], next_id).start()
             z_copy(2, head, index, lse_out.at[head, index], lse_in.at[head, index], next_id).start()
 
-    def near(head, slope):
-        for index in range(blocks):
-            first = index * BLOCK
+    def near_weigh(head, slope):
+        for index in range(blocks):
+            first, place = index * BLOCK, near_place(index)
             scores, allowed = score(head, first, first, BLOCK, slope, 0.0)
             causal = lax.broadcasted_iota(jnp.int32, (BLOCK, BLOCK), 0) <= (
                 lax.broadcasted_iota(jnp.int32, (BLOCK, BLOCK), 1)
             )
-            pieces = [(first, BLOCK, jnp.where(allowed & causal, scores, NEG_FILL))]
+            pieces = [(place + first, BLOCK, jnp.where(allowed & causal, scores, NEG_FILL))]
             if index:
                 scores, allowed = score(head, first, 0, first, slope, 0.0)
-                pieces.append((0, first, jnp.where(allowed, scores, NEG_FILL)))
+                pieces.append((place, first, jnp.where(allowed, scores, NEG_FILL)))
             row_max = functools.reduce(
                 jnp.maximum, [jnp.max(piece, axis=0, keepdims=True) for _, _, piece in pieces]
             )
-            row_total, total = 0.0, 0.0
-            for key_first, key_count, piece in pieces:
+            row_total = 0.0
+            for piece_first, count, piece in pieces:
                 weights = jnp.exp2(piece - row_max)
                 row_total = row_total + jnp.sum(weights, axis=0, keepdims=True)
-                total = total + weighted(key_first, key_count, weights)
-            near_sum[:, pl.ds(first, BLOCK)] = total
-            near_max[:, pl.ds(first, BLOCK)] = row_max
-            near_total[:, pl.ds(first, BLOCK)] = row_total
+                near_weights[pl.ds(piece_first, count), :] = weights.astype(near_weights.dtype)
+            near_max[head, :, pl.ds(first, BLOCK)] = row_max
+            near_total[head, :, pl.ds(first, BLOCK)] = row_total
+
+    def near_add():
+        for index in range(blocks):
+            count = (index + 1) * BLOCK
+            weights = near_weights[pl.ds(near_place(index), count), :]
+            near_sum[:, pl.ds(index * BLOCK, BLOCK)] = weighted(0, count, weights)
 
     def send_home(head, index):
         for part in range(BLOCK // rows):
@@ -193,7 +216,7 @@
                     done_rows, out_ref.at[:, columns(slot, head)], out_recv
                 ).start()
 
-    def finish(head, send):
+    def finish(head):
         for index in range(blocks):
             part = pl.ds(index * BLOCK, BLOCK)
 
@@ -202,21 +225,20 @@
                 whole(far_in.at[head, index], z_recv.at[1, head, index]).wait()
                 whole(lse_in.at[head, index], z_recv.at[2, head, index]).wait()
                 far_lse = lse_in[head, index]
-                top = jnp.maximum(near_max[:, part], far_lse)
-                near_scale = jnp.exp2(near_max[:, part] - top)
+                top = jnp.maximum(near_max[head, :, part], far_lse)
+                near_scale = jnp.exp2(near_max[head, :, part] - top)
                 far_scale = jnp.exp2(far_lse - top)
-                inverse = 1.0 / (near_total[:, part] * near_scale + far_scale)
+                inverse = 1.0 / (near_total[head, :, part] * near_scale + far_scale)
                 merged = near_sum[:, part] * (near_scale * inverse)
                 merged = merged + far_in[head, index].astype(jnp.float32) * (far_scale * inverse)
                 o_buf[head, part, :] = merged.T.astype(o_buf.dtype)
 
             @pl.when(jnp.logical_not(has_prev))
             def _():
-                alone = near_sum[:, part] / near_total[:, part]
+                alone = near_sum[:, part] / near_total[head, :, part]
                 o_buf[head, part, :] = alone.T.astype(o_buf.dtype)
 
-            if send:
-                send_home(head, index)
+            send_home(head, index)
 
     def queries_back(head, unused):
         whole(q_buf.at[head, pl.ds(0, DOC_MAX), :], in_recv.at[0, head]).wait()
@@ -237,38 +259,29 @@
     def one_head(head, unused):
         slope = slope_ref[slot * heads + head] * LOG2E
         whole(k_buf.at[head], in_recv.at[1, head]).wait()
+
+        @pl.when(has_next)
+        def _():
+            whole(q_buf.at[head, pl.ds(DOC_MAX, DOC_MAX), :], z_recv.at[0, head, 0]).wait()
+            far_weigh(head, slope)
+
+        near_weigh(head, slope)
         whole(v_buf.at[head], in_recv.at[2, head]).wait()
-
-        @pl.when(head == heads - 1)
-        def _():
-            def send_early(early, unused):
-                for index in range(blocks):
-                    send_home(early, index)
-                return unused
-
-            lax.fori_loop(0, heads - 2, send_early, 0)
-
         vt_buf[...] = v_buf[head].T
 
         @pl.when(has_next)
         def _():
-            whole(q_buf.at[head, pl.ds(DOC_MAX, DOC_MAX), :], z_recv.at[0, head, 0]).wait()
-            far(head, slope)
+            far_send(head)
 
         @pl.when(head > 0)
         def _():
-            finish(head - 1, False)
-
-        @pl.when(head == heads - 1)
-        def _():
-            for index in range(blocks):
-                send_home(heads - 2, index)
-
-        near(head, slope)
+            finish(head - 1)
+
+        near_add()
         return unused
 
     lax.fori_loop(0, heads, one_head, 0)
-    finish(heads - 1, True)
+    finish(heads - 1)
 
     sent = pl.ds(0, (slots - 1) * heads * width)
     for kind, source in enumerate((q_ref, k_ref, v_ref)):
@@ -317,7 +330,10 @@
             pltpu.VMEM((heads, blocks, 1, BLOCK), jnp.float32),
             pltpu.VMEM((heads, blocks, 1, BLOCK), jnp.float32),
             pltpu.VMEM((width, DOC_MAX), jnp.float32),
-            pltpu.VMEM((1, DOC_MAX), jnp.float32),
+            pltpu.VMEM((heads, 1, DOC_MAX), jnp.float32),
+            pltpu.VMEM((heads, 1, DOC_MAX), jnp.float32),
+            pltpu.VMEM((blocks * (blocks + 1) // 2 * BLOCK, BLOCK), dtype),
+            pltpu.VMEM((blocks * (blocks + 1) // 2 * BLOCK, BLOCK), dtype),
             pltpu.VMEM((1, DOC_MAX), jnp.float32),
             pltpu.VMEM((1, 2 * DOC_MAX), jnp.float32),
             pltpu.VMEM((DOC_MAX, BLOCK), jnp.float32),

time: 55.9 us -> 53.7 us (0.961)
  the two profiles are of different devices: /device:TPU:1 before, /device:TPU:31 now
where the time goes in v1:
time: 53.7 us; the launch traced here: 52.9 us
  Pallas kernels  50.6 us (94%)
  local copies, waits for them, and re-layouts  2.29 us (4%)
    pallas_call x1, Pallas kernels, per_device(): pl.pallas_call(functools.partial(kernel, plane_groups, inner_count, plane...  50.6 us
    unnamed x1, local copies, waits for them, and re-layouts  2.29 us

profile of v1, /device:TPU:31, one launch (start us, length us, event | category | flops | bytes accessed | tf_op | source)
XLA Modules:
  0.0 52.9 jit_solution(10710549221173158735)
XLA Ops:
  0.0 50.6 %shard_map.55 = bf16[128,4096]{1,0:T(8,128)(2,1)} custom-call(s32[8]{0:T(128)} %doc_hbm.1, f32[32]{0:T(128)} %slope_hbm.1, bf16[128,4096]{1,0:T(8,128)(2,1)} %q_ref.1, bf16[128,4096]{1,0:T(8,128)(2,1)} %k_ref.1, bf16[128,4096]{1,0:T(8,128)(2,1)} %v_ref.1), custom_call_target="tpu_custom_call" | custom-call | flops 2684354560 | bytes 4194304 | tf_op jit(solution)/shard_map/pallas_call | solution.py:315
  50.6 2.3 %copy.7 = bf16[128,4096]{1,0:T(8,128)(2,1)} copy(bf16[128,4096]{1,0:T(8,128)(2,1)} %shard_map.55) | data formatting | bytes 2097152
